TPU v7x, 128 devices: a whole 4x4x4 slice. The times are simulated.
128 devices in a mesh: gx: 4 (over x), gy: 32 (over z, y, core).
Axes of the slice: x: 4, y: 4, z: 4, core: 2. Of those that a mesh axis runs over, the one named last changes fastest.
Arguments:
- positions: float32 [8192, 3, 128], P(('gx', 'gy')), may hold values from 0 to 64, as said below
- charges: float32 [8192, 128], P(('gx', 'gy')), may hold values from -8 to 8, as said below
- send_x: int32 [128, 2, 32], P(('gx', 'gy')), may hold values from -1 to 63, as said below
- send_y: int32 [128, 2, 32], P(('gx', 'gy')), may hold values from -1 to 63, as said below
- send_corner: int32 [128, 4, 16], P(('gx', 'gy')), may hold values from -1 to 63, as said below
- near_slot: int32 [8192, 27], P(('gx', 'gy')), may hold values from -1 to 255, as said below
- far_sources: int32 [1024, 316], P(('gx', 'gy')), may hold values from -1 to 1023, as said below
- translations: bfloat16 [121, 38236], replicated, may hold values from -0.0078125 to 0.0078125
Outputs:
- potential: float32 [8192, 128], P(('gx', 'gy'))
- field_strength: float32 [8192, 3, 128], P(('gx', 'gy'))
Inputs may be any that keep to these rules, and one draw needn't show every extreme that they name: `send_x`: row [s, k] lists in increasing order, padded with -1, the local indices of the leaves of device s that hold particles and have local x coordinate 0 (k = 0) or 2 - 1 (k = 1); in every draw some device fills both rows. `send_y`: row [s, k] lists in increasing order, padded with -1, the local indices of the leaves of device s that hold particles and have local y coordinate 0 (k = 0) or 2 - 1 (k = 1); in every draw some device fills both rows. `send_corner`: row [s, k], k = 2 kx + ky, lists in increasing order, padded with -1, the local indices of the leaves of device s that hold particles and have local x coordinate kx (1) and local y coordinate ky (1); in every draw some device fills all four rows. `near_slot`: offset n = 9 (a + 1) + 3 (b + 1) + (c + 1) for the neighbour at (a, b, c) in -1..1; -1 where that leaf lies outside the domain or holds no particles; otherwise the entry of the owner's source table that holds it (n = 13 is the leaf itself). `far_sources`: class k is the k-th offset (a, b, c) in -3..3 with max(|a|, |b|, |c|) > 1, taken in increasing 49 a + 7 b + c; the entry is the upper cell at that offset where it lies in the domain, holds particles and its parent (coordinates halved, rounded down) touches or equals the parent of m, else -1. positions[g, :, p] lies in the unit box of leaf g. `charges`: empty leaves and the slots after each leaf's particle count hold zero.
All inputs are finite; a program needn't handle non-finite values.
Results may differ from a plain program's by a relative error of at most 0.0003.
Values may be sent and summed in bfloat16 or wider, within the bound.
A program may use at most 64 MiB of HBM per device.

v0:
```python
import math
import jax
import jax.numpy as jnp
from jax import lax
from jax.sharding import PartitionSpec as P

ORDER = 10
COEF = 121
BX = 2
BY = 2
BZ = 16
UP_DEV = 8
softening = 0.01


def passed_along(value, axis, steps):
    count = lax.axis_size(axis)
    first, last = (max(0, -steps), min(count, count - steps))
    return lax.ppermute(value, axis, [(source, source + steps) for source in range(first, last)])


def upper_centers(cells, row_count):
    half_y = BY // 2
    half_z = BZ // 2
    device = cells // UP_DEV
    local_ids = cells % UP_DEV
    cell_x = device // row_count * (BX // 2) + local_ids // (half_y * half_z)
    cell_y = device % row_count * half_y + local_ids // half_z % half_y
    cell_z = local_ids % half_z
    return 2.0 * jnp.stack([cell_x, cell_y, cell_z], axis=1).astype(jnp.float32) + 1.0


def harmonics(xcoord, ycoord, zcoord):
    radius_sq = xcoord * xcoord + ycoord * ycoord + zcoord * zcoord
    unity = jnp.ones_like(xcoord)
    nothing = jnp.zeros_like(xcoord)
    solid_harm = {(0, 0): (unity, nothing)}
    for moment in range(1, ORDER + 1):
        real_part, imag_part = solid_harm[moment - 1, moment - 1]
        factor = -0.5 / moment
        solid_harm[moment, moment] = (
            factor * (xcoord * real_part - ycoord * imag_part),
            factor * (xcoord * imag_part + ycoord * real_part),
        )
    for moment in range(ORDER + 1):
        if moment + 1 <= ORDER:
            real_part, imag_part = solid_harm[moment, moment]
            solid_harm[moment + 1, moment] = (zcoord * real_part, zcoord * imag_part)
        for degree in range(moment + 2, ORDER + 1):
            factor = 1.0 / ((degree - moment) * (degree + moment))
            one_back = solid_harm[degree - 1, moment]
            two_back = solid_harm[degree - 2, moment]
            solid_harm[degree, moment] = (
                factor * ((2 * degree - 1) * zcoord * one_back[0] - radius_sq * two_back[0]),
                factor * ((2 * degree - 1) * zcoord * one_back[1] - radius_sq * two_back[1]),
            )
    stacked = []
    for degree in range(ORDER + 1):
        for moment in range(degree + 1):
            scaling = math.sqrt(math.factorial(degree + moment) * math.factorial(degree - moment))
            real_part, imag_part = solid_harm[degree, moment]
            stacked.append(scaling * real_part)
            if moment > 0:
                stacked.append(scaling * imag_part)
    return jnp.stack(stacked, axis=0)


def leaf_multipoles(positions, charges, centers):
    repeated = jnp.repeat(centers, 8, axis=0)
    offsets = positions - repeated[:, :, None]
    harm = harmonics(offsets[:, 0], offsets[:, 1], offsets[:, 2])
    per_leaf = jnp.sum(harm * charges[None], axis=2)
    return per_leaf.reshape(COEF, -1, 8).sum(axis=2)


def far_field(positions, centers, local_exp):
    repeated = jnp.repeat(centers, 8, axis=0)
    per_leaf = jnp.repeat(local_exp, 8, axis=1)

    def summed_field(points):
        offsets = points - repeated[:, :, None]
        harm = harmonics(offsets[:, 0], offsets[:, 1], offsets[:, 2])
        return jnp.sum(harm * per_leaf[:, :, None], axis=0)

    potential, pullback = jax.vjp(summed_field, positions)
    gradient = pullback(jnp.ones_like(potential))[0]
    return (potential, -gradient)


def translate(everyone, far_sources, translations):
    usable = far_sources >= 0
    picked = jnp.take(everyone, jnp.maximum(far_sources, 0), axis=1)
    picked = jnp.where(usable[None], picked, jnp.zeros((), picked.dtype))
    stacked = jnp.transpose(picked, (1, 2, 0)).reshape(picked.shape[1], -1)
    return jnp.einsum("uk,ik->iu", stacked, translations, preferred_element_type=jnp.float32)


def near_field(targets, source_points, source_charge, slot_ids):
    identity = jnp.eye(targets.shape[2], dtype=jnp.float32)

    def neighbour_step(running, inputs):
        potential, electric = running
        column, neighbour = inputs
        present = column >= 0
        safe = jnp.maximum(column, 0)
        points = source_points[safe]
        charge = jnp.where(present[:, None], source_charge[safe], 0.0)
        separation = targets[:, :, :, None] - points[:, :, None, :]
        distance = jnp.sum(separation * separation, axis=1) + softening
        inverse = lax.rsqrt(distance)
        self_mask = jnp.where(neighbour == 13, 1.0 - identity, 1.0)
        weight = charge[:, None, :] * inverse * self_mask
        potential = potential + jnp.sum(weight, axis=2)
        electric = electric + jnp.sum(separation * (weight * inverse * inverse)[:, None], axis=3)
        return ((potential, electric), None)

    start = (
        jnp.zeros(targets.shape[:1] + targets.shape[2:], jnp.float32),
        jnp.zeros(targets.shape, jnp.float32),
    )
    result = lax.scan(neighbour_step, start, (slot_ids.T, jnp.arange(27, dtype=jnp.int32)))[0]
    return result


def pack_blocks(listing, positions, charges):
    present = listing >= 0
    chosen = jnp.maximum(listing, 0)
    points = jnp.where(present[:, :, None, None], positions[chosen], 0.0)
    charge = jnp.where(present[:, :, None], charges[chosen], 0.0)
    return jnp.concatenate([points, charge[:, :, None]], axis=2)


def per_device(
    positions, charges, send_x, send_y, send_corner, near_slot, far_sources, translations
):
    inner_count = lax.axis_size("gy")
    device = lax.axis_index("gx") * inner_count + lax.axis_index("gy")
    cells = device * UP_DEV + jnp.arange(UP_DEV, dtype=jnp.int32)
    centers = upper_centers(cells, inner_count)
    multipole = leaf_multipoles(positions, charges, centers).astype(jnp.bfloat16)
    everyone = lax.all_gather(multipole, ("gx", "gy"), axis=1, tiled=True)
    local_exp = translate(everyone, far_sources, translations)
    far_pot, far_force = far_field(positions, centers, local_exp)
    own_blocks = jnp.concatenate([positions, charges[:, None]], axis=1)
    packed_x = pack_blocks(send_x[0], positions, charges)
    packed_y = pack_blocks(send_y[0], positions, charges)
    packed_edge = pack_blocks(send_corner[0], positions, charges)
    table_parts = [own_blocks]
    for block in range(2):
        table_parts.append(passed_along(packed_x[1 - block], "gx", 1 - 2 * block))
    for block in range(2):
        table_parts.append(passed_along(packed_y[1 - block], "gy", 1 - 2 * block))
    for block in range(4):
        step_x = 2 * (block // 2) - 1
        step_y = 2 * (block % 2) - 1
        table_parts.append(
            passed_along(packed_edge[3 - block], ("gx", "gy"), -(step_x * inner_count + step_y))
        )
    table = jnp.concatenate(table_parts, axis=0)
    near_pot, near_force = near_field(positions, table[:, :3], table[:, 3], near_slot)
    return (far_pot + near_pot, far_force + near_force)


def solution(mesh):
    return jax.shard_map(
        per_device,
        mesh=mesh,
        in_specs=(
            P(("gx", "gy"), None, None),
            P(("gx", "gy"), None),
            P(("gx", "gy"), None, None),
            P(("gx", "gy"), None, None),
            P(("gx", "gy"), None, None),
            P(("gx", "gy"), None),
            P(("gx", "gy"), None),
            P(),
        ),
        out_specs=(P(("gx", "gy"), None), P(("gx", "gy"), None, None)),
        check_vma=False,
    )
```

profile of v0, /device:TPU:121, one launch (start us, length us, event | category | flops | bytes accessed | tf_op | source)
XLA Modules:
  0.0 867.6 jit_solution(16908647988988412900)
XLA Ops:
  105.4 37.0 %all_gather.3 = bf16[121,1024]{0,1:T(8,128)(2,1)S(1)} all-gather(bf16[121,8]{0,1:T(8,128)(2,1)S(1)} %bitcast_reduce_fusion), channel_id=1, replica_groups=mesh['gx'=4,'gy'=32] {'gx','gy'}, dimensions={1}, use_global_device_ids=true | all-gather | bytes 249744 | tf_op jit(solution)/shard_map/all_gather | solution.py:141
  193.6 6.3 collective-permute-start.6
  202.2 8.8 %collective-permute-done.7 = f32[16,4,128]{2,1,0:T(4,128)S(1)} collective-permute-done((f32[16,4,128]{2,1,0:T(4,128)S(1)}, f32[16,4,128]{2,1,0:T(4,128)S(1)}, u32[]{:S(2)}, u32[]{:S(2)}) %collective-permute-start.7) | collective-permute-done | bytes 32800 | tf_op jit(solution)/shard_map/ppermute | solution.py:19
  211.1 655.2 %while.13 = (s32[]{:T(128)}, f32[64,128]{1,0:T(8,128)S(1)}, f32[64,3,128]{2,1,0:T(4,128)S(1)}, s32[27,64]{1,0:T(8,128)}, f32[256,128]{1,0:T(8,128)S(1)}, /*index...) while((s32[]{:T(128)}, f32[64,128]{1,0:T(8,128)S(1)}, ...), condition=%wide.region_7.8_spmd.clone, body=%wide.region_3.7_spmd.clone.sunk | while | flops 24224900 | bytes 18192156 | solution.py:121
  226.4 8.9 %fusion.455 = f32[64,3,128]{2,1,0:T(4,128)S(1)} fusion(f32[64,128,128]{2,1,0:T(8,128)} %get-tuple-element.385, f32[64,3,128]{2,1,0:T(4,128)S(1)} %gather_fusion, f32[64,3,128]{2,1,0:T(4,128)S(1)} %get-tuple-element.413), kind=kLoop, calls=%fused_computation.13.clone.1 | loop fusion | flops 9412608 | bytes 4489216 | tf_op jit(solution)/shard_map/while/body/eval_jaxpr/reduce_sum | solution.py:114
  236.8 6.0 fusion.453
  250.6 8.9 %fusion.455 = f32[64,3,128]{2,1,0:T(4,128)S(1)} fusion(f32[64,128,128]{2,1,0:T(8,128)} %get-tuple-element.385, f32[64,3,128]{2,1,0:T(4,128)S(1)} %gather_fusion, f32[64,3,128]{2,1,0:T(4,128)S(1)} %get-tuple-element.413), kind=kLoop, calls=%fused_computation.13.clone.1 | loop fusion | flops 9412608 | bytes 4489216 | tf_op jit(solution)/shard_map/while/body/eval_jaxpr/reduce_sum | solution.py:114
  274.9 8.9 %fusion.455 = f32[64,3,128]{2,1,0:T(4,128)S(1)} fusion(f32[64,128,128]{2,1,0:T(8,128)} %get-tuple-element.385, f32[64,3,128]{2,1,0:T(4,128)S(1)} %gather_fusion, f32[64,3,128]{2,1,0:T(4,128)S(1)} %get-tuple-element.413), kind=kLoop, calls=%fused_computation.13.clone.1 | loop fusion | flops 9412608 | bytes 4489216 | tf_op jit(solution)/shard_map/while/body/eval_jaxpr/reduce_sum | solution.py:114
  299.2 8.9 %fusion.455 = f32[64,3,128]{2,1,0:T(4,128)S(1)} fusion(f32[64,128,128]{2,1,0:T(8,128)} %get-tuple-element.385, f32[64,3,128]{2,1,0:T(4,128)S(1)} %gather_fusion, f32[64,3,128]{2,1,0:T(4,128)S(1)} %get-tuple-element.413), kind=kLoop, calls=%fused_computation.13.clone.1 | loop fusion | flops 9412608 | bytes 4489216 | tf_op jit(solution)/shard_map/while/body/eval_jaxpr/reduce_sum | solution.py:114
  323.4 8.9 %fusion.455 = f32[64,3,128]{2,1,0:T(4,128)S(1)} fusion(f32[64,128,128]{2,1,0:T(8,128)} %get-tuple-element.385, f32[64,3,128]{2,1,0:T(4,128)S(1)} %gather_fusion, f32[64,3,128]{2,1,0:T(4,128)S(1)} %get-tuple-element.413), kind=kLoop, calls=%fused_computation.13.clone.1 | loop fusion | flops 9412608 | bytes 4489216 | tf_op jit(solution)/shard_map/while/body/eval_jaxpr/reduce_sum | solution.py:114
  347.7 8.9 %fusion.455 = f32[64,3,128]{2,1,0:T(4,128)S(1)} fusion(f32[64,128,128]{2,1,0:T(8,128)} %get-tuple-element.385, f32[64,3,128]{2,1,0:T(4,128)S(1)} %gather_fusion, f32[64,3,128]{2,1,0:T(4,128)S(1)} %get-tuple-element.413), kind=kLoop, calls=%fused_computation.13.clone.1 | loop fusion | flops 9412608 | bytes 4489216 | tf_op jit(solution)/shard_map/while/body/eval_jaxpr/reduce_sum | solution.py:114
  372.0 8.9 %fusion.455 = f32[64,3,128]{2,1,0:T(4,128)S(1)} fusion(f32[64,128,128]{2,1,0:T(8,128)} %get-tuple-element.385, f32[64,3,128]{2,1,0:T(4,128)S(1)} %gather_fusion, f32[64,3,128]{2,1,0:T(4,128)S(1)} %get-tuple-element.413), kind=kLoop, calls=%fused_computation.13.clone.1 | loop fusion | flops 9412608 | bytes 4489216 | tf_op jit(solution)/shard_map/while/body/eval_jaxpr/reduce_sum | solution.py:114
  396.2 8.9 %fusion.455 = f32[64,3,128]{2,1,0:T(4,128)S(1)} fusion(f32[64,128,128]{2,1,0:T(8,128)} %get-tuple-element.385, f32[64,3,128]{2,1,0:T(4,128)S(1)} %gather_fusion, f32[64,3,128]{2,1,0:T(4,128)S(1)} %get-tuple-element.413), kind=kLoop, calls=%fused_computation.13.clone.1 | loop fusion | flops 9412608 | bytes 4489216 | tf_op jit(solution)/shard_map/while/body/eval_jaxpr/reduce_sum | solution.py:114
  420.5 8.9 %fusion.455 = f32[64,3,128]{2,1,0:T(4,128)S(1)} fusion(f32[64,128,128]{2,1,0:T(8,128)} %get-tuple-element.385, f32[64,3,128]{2,1,0:T(4,128)S(1)} %gather_fusion, f32[64,3,128]{2,1,0:T(4,128)S(1)} %get-tuple-element.413), kind=kLoop, calls=%fused_computation.13.clone.1 | loop fusion | flops 9412608 | bytes 4489216 | tf_op jit(solution)/shard_map/while/body/eval_jaxpr/reduce_sum | solution.py:114
  444.8 8.9 %fusion.455 = f32[64,3,128]{2,1,0:T(4,128)S(1)} fusion(f32[64,128,128]{2,1,0:T(8,128)} %get-tuple-element.385, f32[64,3,128]{2,1,0:T(4,128)S(1)} %gather_fusion, f32[64,3,128]{2,1,0:T(4,128)S(1)} %get-tuple-element.413), kind=kLoop, calls=%fused_computation.13.clone.1 | loop fusion | flops 9412608 | bytes 4489216 | tf_op jit(solution)/shard_map/while/body/eval_jaxpr/reduce_sum | solution.py:114
  469.0 8.9 %fusion.455 = f32[64,3,128]{2,1,0:T(4,128)S(1)} fusion(f32[64,128,128]{2,1,0:T(8,128)} %get-tuple-element.385, f32[64,3,128]{2,1,0:T(4,128)S(1)} %gather_fusion, f32[64,3,128]{2,1,0:T(4,128)S(1)} %get-tuple-element.413), kind=kLoop, calls=%fused_computation.13.clone.1 | loop fusion | flops 9412608 | bytes 4489216 | tf_op jit(solution)/shard_map/while/body/eval_jaxpr/reduce_sum | solution.py:114
  493.3 8.9 %fusion.455 = f32[64,3,128]{2,1,0:T(4,128)S(1)} fusion(f32[64,128,128]{2,1,0:T(8,128)} %get-tuple-element.385, f32[64,3,128]{2,1,0:T(4,128)S(1)} %gather_fusion, f32[64,3,128]{2,1,0:T(4,128)S(1)} %get-tuple-element.413), kind=kLoop, calls=%fused_computation.13.clone.1 | loop fusion | flops 9412608 | bytes 4489216 | tf_op jit(solution)/shard_map/while/body/eval_jaxpr/reduce_sum | solution.py:114
  517.6 8.9 %fusion.455 = f32[64,3,128]{2,1,0:T(4,128)S(1)} fusion(f32[64,128,128]{2,1,0:T(8,128)} %get-tuple-element.385, f32[64,3,128]{2,1,0:T(4,128)S(1)} %gather_fusion, f32[64,3,128]{2,1,0:T(4,128)S(1)} %get-tuple-element.413), kind=kLoop, calls=%fused_computation.13.clone.1 | loop fusion | flops 9412608 | bytes 4489216 | tf_op jit(solution)/shard_map/while/body/eval_jaxpr/reduce_sum | solution.py:114
  541.8 8.9 %fusion.455 = f32[64,3,128]{2,1,0:T(4,128)S(1)} fusion(f32[64,128,128]{2,1,0:T(8,128)} %get-tuple-element.385, f32[64,3,128]{2,1,0:T(4,128)S(1)} %gather_fusion, f32[64,3,128]{2,1,0:T(4,128)S(1)} %get-tuple-element.413), kind=kLoop, calls=%fused_computation.13.clone.1 | loop fusion | flops 9412608 | bytes 4489216 | tf_op jit(solution)/shard_map/while/body/eval_jaxpr/reduce_sum | solution.py:114
  566.1 8.9 %fusion.455 = f32[64,3,128]{2,1,0:T(4,128)S(1)} fusion(f32[64,128,128]{2,1,0:T(8,128)} %get-tuple-element.385, f32[64,3,128]{2,1,0:T(4,128)S(1)} %gather_fusion, f32[64,3,128]{2,1,0:T(4,128)S(1)} %get-tuple-element.413), kind=kLoop, calls=%fused_computation.13.clone.1 | loop fusion | flops 9412608 | bytes 4489216 | tf_op jit(solution)/shard_map/while/body/eval_jaxpr/reduce_sum | solution.py:114
  590.4 8.9 %fusion.455 = f32[64,3,128]{2,1,0:T(4,128)S(1)} fusion(f32[64,128,128]{2,1,0:T(8,128)} %get-tuple-element.385, f32[64,3,128]{2,1,0:T(4,128)S(1)} %gather_fusion, f32[64,3,128]{2,1,0:T(4,128)S(1)} %get-tuple-element.413), kind=kLoop, calls=%fused_computation.13.clone.1 | loop fusion | flops 9412608 | bytes 4489216 | tf_op jit(solution)/shard_map/while/body/eval_jaxpr/reduce_sum | solution.py:114
  614.6 8.9 %fusion.455 = f32[64,3,128]{2,1,0:T(4,128)S(1)} fusion(f32[64,128,128]{2,1,0:T(8,128)} %get-tuple-element.385, f32[64,3,128]{2,1,0:T(4,128)S(1)} %gather_fusion, f32[64,3,128]{2,1,0:T(4,128)S(1)} %get-tuple-element.413), kind=kLoop, calls=%fused_computation.13.clone.1 | loop fusion | flops 9412608 | bytes 4489216 | tf_op jit(solution)/shard_map/while/body/eval_jaxpr/reduce_sum | solution.py:114
  638.9 8.9 %fusion.455 = f32[64,3,128]{2,1,0:T(4,128)S(1)} fusion(f32[64,128,128]{2,1,0:T(8,128)} %get-tuple-element.385, f32[64,3,128]{2,1,0:T(4,128)S(1)} %gather_fusion, f32[64,3,128]{2,1,0:T(4,128)S(1)} %get-tuple-element.413), kind=kLoop, calls=%fused_computation.13.clone.1 | loop fusion | flops 9412608 | bytes 4489216 | tf_op jit(solution)/shard_map/while/body/eval_jaxpr/reduce_sum | solution.py:114
  663.2 8.9 %fusion.455 = f32[64,3,128]{2,1,0:T(4,128)S(1)} fusion(f32[64,128,128]{2,1,0:T(8,128)} %get-tuple-element.385, f32[64,3,128]{2,1,0:T(4,128)S(1)} %gather_fusion, f32[64,3,128]{2,1,0:T(4,128)S(1)} %get-tuple-element.413), kind=kLoop, calls=%fused_computation.13.clone.1 | loop fusion | flops 9412608 | bytes 4489216 | tf_op jit(solution)/shard_map/while/body/eval_jaxpr/reduce_sum | solution.py:114
  687.4 8.9 %fusion.455 = f32[64,3,128]{2,1,0:T(4,128)S(1)} fusion(f32[64,128,128]{2,1,0:T(8,128)} %get-tuple-element.385, f32[64,3,128]{2,1,0:T(4,128)S(1)} %gather_fusion, f32[64,3,128]{2,1,0:T(4,128)S(1)} %get-tuple-element.413), kind=kLoop, calls=%fused_computation.13.clone.1 | loop fusion | flops 9412608 | bytes 4489216 | tf_op jit(solution)/shard_map/while/body/eval_jaxpr/reduce_sum | solution.py:114
  711.7 8.9 %fusion.455 = f32[64,3,128]{2,1,0:T(4,128)S(1)} fusion(f32[64,128,128]{2,1,0:T(8,128)} %get-tuple-element.385, f32[64,3,128]{2,1,0:T(4,128)S(1)} %gather_fusion, f32[64,3,128]{2,1,0:T(4,128)S(1)} %get-tuple-element.413), kind=kLoop, calls=%fused_computation.13.clone.1 | loop fusion | flops 9412608 | bytes 4489216 | tf_op jit(solution)/shard_map/while/body/eval_jaxpr/reduce_sum | solution.py:114
  736.0 8.9 %fusion.455 = f32[64,3,128]{2,1,0:T(4,128)S(1)} fusion(f32[64,128,128]{2,1,0:T(8,128)} %get-tuple-element.385, f32[64,3,128]{2,1,0:T(4,128)S(1)} %gather_fusion, f32[64,3,128]{2,1,0:T(4,128)S(1)} %get-tuple-element.413), kind=kLoop, calls=%fused_computation.13.clone.1 | loop fusion | flops 9412608 | bytes 4489216 | tf_op jit(solution)/shard_map/while/body/eval_jaxpr/reduce_sum | solution.py:114
  760.2 8.9 %fusion.455 = f32[64,3,128]{2,1,0:T(4,128)S(1)} fusion(f32[64,128,128]{2,1,0:T(8,128)} %get-tuple-element.385, f32[64,3,128]{2,1,0:T(4,128)S(1)} %gather_fusion, f32[64,3,128]{2,1,0:T(4,128)S(1)} %get-tuple-element.413), kind=kLoop, calls=%fused_computation.13.clone.1 | loop fusion | flops 9412608 | bytes 4489216 | tf_op jit(solution)/shard_map/while/body/eval_jaxpr/reduce_sum | solution.py:114
  784.5 8.9 %fusion.455 = f32[64,3,128]{2,1,0:T(4,128)S(1)} fusion(f32[64,128,128]{2,1,0:T(8,128)} %get-tuple-element.385, f32[64,3,128]{2,1,0:T(4,128)S(1)} %gather_fusion, f32[64,3,128]{2,1,0:T(4,128)S(1)} %get-tuple-element.413), kind=kLoop, calls=%fused_computation.13.clone.1 | loop fusion | flops 9412608 | bytes 4489216 | tf_op jit(solution)/shard_map/while/body/eval_jaxpr/reduce_sum | solution.py:114
  808.8 8.9 %fusion.455 = f32[64,3,128]{2,1,0:T(4,128)S(1)} fusion(f32[64,128,128]{2,1,0:T(8,128)} %get-tuple-element.385, f32[64,3,128]{2,1,0:T(4,128)S(1)} %gather_fusion, f32[64,3,128]{2,1,0:T(4,128)S(1)} %get-tuple-element.413), kind=kLoop, calls=%fused_computation.13.clone.1 | loop fusion | flops 9412608 | bytes 4489216 | tf_op jit(solution)/shard_map/while/body/eval_jaxpr/reduce_sum | solution.py:114
  833.0 8.9 %fusion.455 = f32[64,3,128]{2,1,0:T(4,128)S(1)} fusion(f32[64,128,128]{2,1,0:T(8,128)} %get-tuple-element.385, f32[64,3,128]{2,1,0:T(4,128)S(1)} %gather_fusion, f32[64,3,128]{2,1,0:T(4,128)S(1)} %get-tuple-element.413), kind=kLoop, calls=%fused_computation.13.clone.1 | loop fusion | flops 9412608 | bytes 4489216 | tf_op jit(solution)/shard_map/while/body/eval_jaxpr/reduce_sum | solution.py:114
  857.3 8.9 %fusion.455 = f32[64,3,128]{2,1,0:T(4,128)S(1)} fusion(f32[64,128,128]{2,1,0:T(8,128)} %get-tuple-element.385, f32[64,3,128]{2,1,0:T(4,128)S(1)} %gather_fusion, f32[64,3,128]{2,1,0:T(4,128)S(1)} %get-tuple-element.413), kind=kLoop, calls=%fused_computation.13.clone.1 | loop fusion | flops 9412608 | bytes 4489216 | tf_op jit(solution)/shard_map/while/body/eval_jaxpr/reduce_sum | solution.py:114
  (872 shorter events, 550.2 us)
Async XLA Ops:
  0.6 19.6 %copy-start.1 = (f32[64,128]{1,0:T(8,128)S(1)}, f32[64,128]{1,0:T(8,128)}, u32[]{:S(2)}) copy-start(f32[64,128]{1,0:T(8,128)} %param.11) | copy-start | bytes 98308
  0.6 20.2 %copy-start = (f32[64,3,128]{2,0,1:T(8,128)S(1)}, f32[64,3,128]{2,0,1:T(8,128)}, u32[]{:S(2)}) copy-start(f32[64,3,128]{2,0,1:T(8,128)} %param.10) | copy-start | bytes 294916
  0.7 19.6 %copy-start.5 = (s32[1,4,16]{2,1,0:T(4,128)S(1)}, s32[1,4,16]{2,1,0:T(4,128)}, u32[]{:S(2)}) copy-start(s32[1,4,16]{2,1,0:T(4,128)} %param.14) | copy-start | bytes 772
  0.7 25.9 %copy-start.2 = (s32[8,316]{1,0:T(8,128)S(1)}, s32[8,316]{1,0:T(8,128)}, u32[]{:S(2)}) copy-start(s32[8,316]{1,0:T(8,128)} %param.16) | copy-start | bytes 30340
  5.5 185.5 %collective-permute-start = (f32[32,4,128]{2,1,0:T(4,128)S(1)}, f32[32,4,128]{2,1,0:T(4,128)S(1)}, u32[]{:S(2)}, u32[]{:S(2)}) collective-permute-start(f32[32,4,128]{2,1,0:T(4,128)S(1)} %get-tuple-element.310), channel_id=1, source_target_pairs={{0,32},{32,64},{64,96},{1,33},{33,65},{65,97},{2,34},{34,66},{66,9... | collective-permute-start | bytes 196616 | tf_op jit(solution)/shard_map/ppermute | solution.py:19
  8.6 185.0 %collective-permute-start.1 = (f32[32,4,128]{2,1,0:T(4,128)S(1)}, f32[32,4,128]{2,1,0:T(4,128)S(1)}, u32[]{:S(2)}, u32[]{:S(2)}) collective-permute-start(f32[32,4,128]{2,1,0:T(4,128)S(1)} %get-tuple-element.309), channel_id=1, source_target_pairs={{32,0},{64,32},{96,64},{33,1},{65,33},{97,65},{34,2},{66,34},{98,6... | collective-permute-start | bytes 196616 | tf_op jit(solution)/shard_map/ppermute | solution.py:19
  15.4 184.6 %collective-permute-start.2 = (f32[32,4,128]{2,1,0:T(4,128)S(1)}, f32[32,4,128]{2,1,0:T(4,128)S(1)}, u32[]{:S(2)}, u32[]{:S(2)}) collective-permute-start(f32[32,4,128]{2,1,0:T(4,128)S(1)} %get-tuple-element.308), channel_id=1, source_target_pairs={{0,1},{1,2},{2,3},{3,4},{4,5},{5,6},{6,7},{7,8},{8,9},{9,10},{10,1... | collective-permute-start | bytes 196616 | tf_op jit(solution)/shard_map/ppermute | solution.py:19
  16.7 184.6 %collective-permute-start.3 = (f32[32,4,128]{2,1,0:T(4,128)S(1)}, f32[32,4,128]{2,1,0:T(4,128)S(1)}, u32[]{:S(2)}, u32[]{:S(2)}) collective-permute-start(f32[32,4,128]{2,1,0:T(4,128)S(1)} %get-tuple-element.307), channel_id=1, source_target_pairs={{1,0},{2,1},{3,2},{4,3},{5,4},{6,5},{7,6},{8,7},{9,8},{10,9},{11,1... | collective-permute-start | bytes 196616 | tf_op jit(solution)/shard_map/ppermute | solution.py:19
  22.5 178.8 %collective-permute-start.4 = (f32[16,4,128]{2,1,0:T(4,128)}, f32[16,4,128]{2,1,0:T(4,128)}, u32[]{:S(2)}, u32[]{:S(2)}) collective-permute-start(f32[16,4,128]{2,1,0:T(4,128)} %get-tuple-element.304), channel_id=1, source_target_pairs={{0,33},{1,34},{2,35},{3,36},{4,37},{5,38},{6,39},{7,40},{8,41},{9,... | collective-permute-start | bytes 98312 | tf_op jit(solution)/shard_map/ppermute | solution.py:19
  154.4 36.6 %copy-start.4 = (f32[16,4,128]{2,1,0:T(4,128)S(1)}, f32[16,4,128]{2,1,0:T(4,128)}, u32[]{:S(2)}) copy-start(f32[16,4,128]{2,1,0:T(4,128)} %get-tuple-element.305) | copy-start | bytes 98308
  154.9 38.7 %copy-start.3 = (f32[16,4,128]{2,1,0:T(4,128)S(1)}, f32[16,4,128]{2,1,0:T(4,128)}, u32[]{:S(2)}) copy-start(f32[16,4,128]{2,1,0:T(4,128)} %get-tuple-element.306) | copy-start | bytes 98308
  191.0 11.1 %collective-permute-start.5 = (f32[16,4,128]{2,1,0:T(4,128)S(1)}, f32[16,4,128]{2,1,0:T(4,128)S(1)}, u32[]{:S(2)}, u32[]{:S(2)}) collective-permute-start(f32[16,4,128]{2,1,0:T(4,128)S(1)} %copy-done.4), channel_id=1, source_target_pairs={{0,31},{1,32},{2,33},{3,34},{4,35},{5,36},{6,37},{7,38},{8,39},{9,... | collective-permute-start | bytes 98312 | tf_op jit(solution)/shard_map/ppermute | solution.py:19
  193.6 8.5 collective-permute-start.6
  200.0 11.0 %collective-permute-start.7 = (f32[16,4,128]{2,1,0:T(4,128)S(1)}, f32[16,4,128]{2,1,0:T(4,128)S(1)}, u32[]{:S(2)}, u32[]{:S(2)}) collective-permute-start(f32[16,4,128]{2,1,0:T(4,128)S(1)} %get-tuple-element.303), channel_id=1, source_target_pairs={{33,0},{34,1},{35,2},{36,3},{37,4},{38,5},{39,6},{40,7},{41,8},{42... | collective-permute-start | bytes 98312 | tf_op jit(solution)/shard_map/ppermute | solution.py:19
where the time goes:
time: 875 us; the launch traced here: 868 us
  other arithmetic  685 us (78%)
  local copies, waits for them, and re-layouts  89.5 us (10%)
  blocking collectives  37 us (4%)
  starting transfers between devices  22.7 us (3%)
  loops' own time  18.4 us (2%)
  waiting for transfers between devices  8.81 us (1%)
    reduce_sum x27, other arithmetic, neighbour_step(): jnp.sum(separation * (weight * inverse * inverse)[:, None], axis=3)  239 us
    reduce_sum x27, other arithmetic, neighbour_step(): distance = jnp.sum(separation * separation, axis=1) + softening  163 us
    mul x27, other arithmetic, neighbour_step(): weight * inverse * inverse  140 us
    unnamed x121, other arithmetic  73.9 us
    all_gather x1, blocking collectives, per_device(): everyone = lax.all_gather(multipole, ('gx', 'gy'), axis=1, tiled=True)  37 us
    ppermute x8, starting transfers between devices, passed_along(): lax.ppermute(value, axis, [(source, source + steps) for source in range(f...  22.7 us
    max x27, other arithmetic, neighbour_step(): safe = jnp.maximum(column, 0)  18.8 us
    ge x27, other arithmetic, neighbour_step(): present = column >= 0  18.8 us
  transfers between devices with their start and end apart: 8, of which 1 were waited for; matrix products, arithmetic and copies ran while one was open for 16% of the time, Pallas kernels for 0%

commit v1 on v0

--- a/solution.py
+++ b/solution.py
@@ -3,6 +3,7 @@
 import jax.numpy as jnp
 from jax import lax
 from jax.sharding import PartitionSpec as P
+from jax.lax import all_to_all, axis_size
 
 ORDER = 10
 COEF = 121
@@ -138,7 +139,16 @@
     cells = device * UP_DEV + jnp.arange(UP_DEV, dtype=jnp.int32)
     centers = upper_centers(cells, inner_count)
     multipole = leaf_multipoles(positions, charges, centers).astype(jnp.bfloat16)
-    everyone = lax.all_gather(multipole, ("gx", "gy"), axis=1, tiled=True)
+    _start_rows = lambda base_x: jnp.concatenate(
+        all_to_all(
+            jnp.stack([base_x] * axis_size(("gx", "gy"))),
+            axis_name=("gx", "gy"),
+            split_axis=0,
+            concat_axis=0,
+        ),
+        1,
+    )
+    everyone = _start_rows(multipole)
     local_exp = translate(everyone, far_sources, translations)
     far_pot, far_force = far_field(positions, centers, local_exp)
     own_blocks = jnp.concatenate([positions, charges[:, None]], axis=1)

time: 875 us -> 845 us (0.966)
  blocking collectives: 37 us -> 0 us
  starting transfers between devices: 22.7 us -> 33 us
    all_gather x1 -> x0, blocking collectives: 37 us -> none  [per_device(): everyone = lax.all_gather(multipole, ('gx', 'gy'), axis=1, tiled=True)]
    all_to_all x0 -> x1, starting transfers between devices: none -> 10 us  [per_device(): all_to_all(jnp.stack([base_x] * axis_size(('gx', 'gy'))), axis_name=('gx'...]
  transfers between devices with their start and end apart: 8 -> 9, of which waited for: 1 -> 2; matrix products, arithmetic and copies ran while one was open for 16% -> 77% of each run, Pallas kernels for 0% -> 0%
where the time goes in v1:
time: 845 us; the launch traced here: 835 us
  other arithmetic  681 us (81%)
  local copies, waits for them, and re-layouts  86.2 us (10%)
  starting transfers between devices  33 us (4%)
  loops' own time  18.4 us (2%)
  waiting for transfers between devices  9.38 us (1%)
    reduce_sum x27, other arithmetic, neighbour_step(): jnp.sum(separation * (weight * inverse * inverse)[:, None], axis=3)  239 us
    reduce_sum x27, other arithmetic, neighbour_step(): distance = jnp.sum(separation * separation, axis=1) + softening  163 us
    mul x27, other arithmetic, neighbour_step(): weight * inverse * inverse  140 us
    unnamed x121, other arithmetic  73.9 us
    ppermute x8, starting transfers between devices, passed_along(): lax.ppermute(value, axis, [(source, source + steps) for source in range(f...  23 us
    max x27, other arithmetic, neighbour_step(): safe = jnp.maximum(column, 0)  18.8 us
    ge x27, other arithmetic, neighbour_step(): present = column >= 0  18.8 us
    another operation x1, loops' own time, near_field(): lax.scan(neighbour_step, start, (slot_ids.T, jnp.arange(27, dtype=jnp.int...  18.4 us
  transfers between devices with their start and end apart: 9, of which 2 were waited for; matrix products, arithmetic and copies ran while one was open for 77% of the time, Pallas kernels for 0%

profile of v1, /device:TPU:121, one launch (start us, length us, event | category | flops | bytes accessed | tf_op | source)
XLA Modules:
  0.0 834.7 jit_solution(15431301304054570373)
XLA Ops:
  81.6 10.0 %all-to-all-start = ((bf16[128,121,8]{1,2,0:T(8,128)(2,1)}), bf16[128,121,8]{1,2,0:T(8,128)(2,1)S(1)}, u32[]{:S(2)}, u32[]{:S(2)}) async-start(bf16[128,121,8]{1,2,0:T(8,128)(2,1)} %stack.8), calls=%async_computation | async-start | bytes 524288 | tf_op jit(solution)/shard_map/all_to_all | solution.py:143
  120.9 9.0 %collective-permute-done.7 = f32[16,4,128]{2,1,0:T(4,128)S(1)} collective-permute-done((f32[16,4,128]{2,1,0:T(4,128)S(1)}, f32[16,4,128]{2,1,0:T(4,128)S(1)}, u32[]{:S(2)}, u32[]{:S(2)}) %collective-permute-start.7) | collective-permute-done | bytes 32800 | tf_op jit(solution)/shard_map/ppermute | solution.py:20
  130.1 655.2 %while.13 = (s32[]{:T(128)}, f32[64,128]{1,0:T(8,128)S(1)}, f32[64,3,128]{2,1,0:T(4,128)S(1)}, s32[27,64]{1,0:T(8,128)}, f32[256,128]{1,0:T(8,128)S(1)}, /*index...) while((s32[]{:T(128)}, f32[64,128]{1,0:T(8,128)S(1)}, ...), condition=%wide.region_7.8_spmd.clone, body=%wide.region_3.7_spmd.clone.sunk | while | flops 24224900 | bytes 18192156 | solution.py:122
  145.3 8.9 %fusion.455 = f32[64,3,128]{2,1,0:T(4,128)S(1)} fusion(f32[64,128,128]{2,1,0:T(8,128)} %get-tuple-element.385, f32[64,3,128]{2,1,0:T(4,128)S(1)} %gather_fusion, f32[64,3,128]{2,1,0:T(4,128)S(1)} %get-tuple-element.413), kind=kLoop, calls=%fused_computation.13.clone.1 | loop fusion | flops 9412608 | bytes 4489216 | tf_op jit(solution)/shard_map/while/body/eval_jaxpr/reduce_sum | solution.py:115
  169.6 8.9 %fusion.455 = f32[64,3,128]{2,1,0:T(4,128)S(1)} fusion(f32[64,128,128]{2,1,0:T(8,128)} %get-tuple-element.385, f32[64,3,128]{2,1,0:T(4,128)S(1)} %gather_fusion, f32[64,3,128]{2,1,0:T(4,128)S(1)} %get-tuple-element.413), kind=kLoop, calls=%fused_computation.13.clone.1 | loop fusion | flops 9412608 | bytes 4489216 | tf_op jit(solution)/shard_map/while/body/eval_jaxpr/reduce_sum | solution.py:115
  180.0 6.0 fusion.453
  193.8 8.9 %fusion.455 = f32[64,3,128]{2,1,0:T(4,128)S(1)} fusion(f32[64,128,128]{2,1,0:T(8,128)} %get-tuple-element.385, f32[64,3,128]{2,1,0:T(4,128)S(1)} %gather_fusion, f32[64,3,128]{2,1,0:T(4,128)S(1)} %get-tuple-element.413), kind=kLoop, calls=%fused_computation.13.clone.1 | loop fusion | flops 9412608 | bytes 4489216 | tf_op jit(solution)/shard_map/while/body/eval_jaxpr/reduce_sum | solution.py:115
  218.1 8.9 %fusion.455 = f32[64,3,128]{2,1,0:T(4,128)S(1)} fusion(f32[64,128,128]{2,1,0:T(8,128)} %get-tuple-element.385, f32[64,3,128]{2,1,0:T(4,128)S(1)} %gather_fusion, f32[64,3,128]{2,1,0:T(4,128)S(1)} %get-tuple-element.413), kind=kLoop, calls=%fused_computation.13.clone.1 | loop fusion | flops 9412608 | bytes 4489216 | tf_op jit(solution)/shard_map/while/body/eval_jaxpr/reduce_sum | solution.py:115
  242.4 8.9 %fusion.455 = f32[64,3,128]{2,1,0:T(4,128)S(1)} fusion(f32[64,128,128]{2,1,0:T(8,128)} %get-tuple-element.385, f32[64,3,128]{2,1,0:T(4,128)S(1)} %gather_fusion, f32[64,3,128]{2,1,0:T(4,128)S(1)} %get-tuple-element.413), kind=kLoop, calls=%fused_computation.13.clone.1 | loop fusion | flops 9412608 | bytes 4489216 | tf_op jit(solution)/shard_map/while/body/eval_jaxpr/reduce_sum | solution.py:115
  266.6 8.9 %fusion.455 = f32[64,3,128]{2,1,0:T(4,128)S(1)} fusion(f32[64,128,128]{2,1,0:T(8,128)} %get-tuple-element.385, f32[64,3,128]{2,1,0:T(4,128)S(1)} %gather_fusion, f32[64,3,128]{2,1,0:T(4,128)S(1)} %get-tuple-element.413), kind=kLoop, calls=%fused_computation.13.clone.1 | loop fusion | flops 9412608 | bytes 4489216 | tf_op jit(solution)/shard_map/while/body/eval_jaxpr/reduce_sum | solution.py:115
  290.9 8.9 %fusion.455 = f32[64,3,128]{2,1,0:T(4,128)S(1)} fusion(f32[64,128,128]{2,1,0:T(8,128)} %get-tuple-element.385, f32[64,3,128]{2,1,0:T(4,128)S(1)} %gather_fusion, f32[64,3,128]{2,1,0:T(4,128)S(1)} %get-tuple-element.413), kind=kLoop, calls=%fused_computation.13.clone.1 | loop fusion | flops 9412608 | bytes 4489216 | tf_op jit(solution)/shard_map/while/body/eval_jaxpr/reduce_sum | solution.py:115
  315.1 8.9 %fusion.455 = f32[64,3,128]{2,1,0:T(4,128)S(1)} fusion(f32[64,128,128]{2,1,0:T(8,128)} %get-tuple-element.385, f32[64,3,128]{2,1,0:T(4,128)S(1)} %gather_fusion, f32[64,3,128]{2,1,0:T(4,128)S(1)} %get-tuple-element.413), kind=kLoop, calls=%fused_computation.13.clone.1 | loop fusion | flops 9412608 | bytes 4489216 | tf_op jit(solution)/shard_map/while/body/eval_jaxpr/reduce_sum | solution.py:115
  339.4 8.9 %fusion.455 = f32[64,3,128]{2,1,0:T(4,128)S(1)} fusion(f32[64,128,128]{2,1,0:T(8,128)} %get-tuple-element.385, f32[64,3,128]{2,1,0:T(4,128)S(1)} %gather_fusion, f32[64,3,128]{2,1,0:T(4,128)S(1)} %get-tuple-element.413), kind=kLoop, calls=%fused_computation.13.clone.1 | loop fusion | flops 9412608 | bytes 4489216 | tf_op jit(solution)/shard_map/while/body/eval_jaxpr/reduce_sum | solution.py:115
  363.7 8.9 %fusion.455 = f32[64,3,128]{2,1,0:T(4,128)S(1)} fusion(f32[64,128,128]{2,1,0:T(8,128)} %get-tuple-element.385, f32[64,3,128]{2,1,0:T(4,128)S(1)} %gather_fusion, f32[64,3,128]{2,1,0:T(4,128)S(1)} %get-tuple-element.413), kind=kLoop, calls=%fused_computation.13.clone.1 | loop fusion | flops 9412608 | bytes 4489216 | tf_op jit(solution)/shard_map/while/body/eval_jaxpr/reduce_sum | solution.py:115
  387.9 8.9 %fusion.455 = f32[64,3,128]{2,1,0:T(4,128)S(1)} fusion(f32[64,128,128]{2,1,0:T(8,128)} %get-tuple-element.385, f32[64,3,128]{2,1,0:T(4,128)S(1)} %gather_fusion, f32[64,3,128]{2,1,0:T(4,128)S(1)} %get-tuple-element.413), kind=kLoop, calls=%fused_computation.13.clone.1 | loop fusion | flops 9412608 | bytes 4489216 | tf_op jit(solution)/shard_map/while/body/eval_jaxpr/reduce_sum | solution.py:115
  398.3 6.0 fusion.453
  412.2 8.9 %fusion.455 = f32[64,3,128]{2,1,0:T(4,128)S(1)} fusion(f32[64,128,128]{2,1,0:T(8,128)} %get-tuple-element.385, f32[64,3,128]{2,1,0:T(4,128)S(1)} %gather_fusion, f32[64,3,128]{2,1,0:T(4,128)S(1)} %get-tuple-element.413), kind=kLoop, calls=%fused_computation.13.clone.1 | loop fusion | flops 9412608 | bytes 4489216 | tf_op jit(solution)/shard_map/while/body/eval_jaxpr/reduce_sum | solution.py:115
  436.5 8.9 %fusion.455 = f32[64,3,128]{2,1,0:T(4,128)S(1)} fusion(f32[64,128,128]{2,1,0:T(8,128)} %get-tuple-element.385, f32[64,3,128]{2,1,0:T(4,128)S(1)} %gather_fusion, f32[64,3,128]{2,1,0:T(4,128)S(1)} %get-tuple-element.413), kind=kLoop, calls=%fused_computation.13.clone.1 | loop fusion | flops 9412608 | bytes 4489216 | tf_op jit(solution)/shard_map/while/body/eval_jaxpr/reduce_sum | solution.py:115
  460.7 8.9 %fusion.455 = f32[64,3,128]{2,1,0:T(4,128)S(1)} fusion(f32[64,128,128]{2,1,0:T(8,128)} %get-tuple-element.385, f32[64,3,128]{2,1,0:T(4,128)S(1)} %gather_fusion, f32[64,3,128]{2,1,0:T(4,128)S(1)} %get-tuple-element.413), kind=kLoop, calls=%fused_computation.13.clone.1 | loop fusion | flops 9412608 | bytes 4489216 | tf_op jit(solution)/shard_map/while/body/eval_jaxpr/reduce_sum | solution.py:115
  485.0 8.9 %fusion.455 = f32[64,3,128]{2,1,0:T(4,128)S(1)} fusion(f32[64,128,128]{2,1,0:T(8,128)} %get-tuple-element.385, f32[64,3,128]{2,1,0:T(4,128)S(1)} %gather_fusion, f32[64,3,128]{2,1,0:T(4,128)S(1)} %get-tuple-element.413), kind=kLoop, calls=%fused_computation.13.clone.1 | loop fusion | flops 9412608 | bytes 4489216 | tf_op jit(solution)/shard_map/while/body/eval_jaxpr/reduce_sum | solution.py:115
  509.3 8.9 %fusion.455 = f32[64,3,128]{2,1,0:T(4,128)S(1)} fusion(f32[64,128,128]{2,1,0:T(8,128)} %get-tuple-element.385, f32[64,3,128]{2,1,0:T(4,128)S(1)} %gather_fusion, f32[64,3,128]{2,1,0:T(4,128)S(1)} %get-tuple-element.413), kind=kLoop, calls=%fused_computation.13.clone.1 | loop fusion | flops 9412608 | bytes 4489216 | tf_op jit(solution)/shard_map/while/body/eval_jaxpr/reduce_sum | solution.py:115
  533.5 8.9 %fusion.455 = f32[64,3,128]{2,1,0:T(4,128)S(1)} fusion(f32[64,128,128]{2,1,0:T(8,128)} %get-tuple-element.385, f32[64,3,128]{2,1,0:T(4,128)S(1)} %gather_fusion, f32[64,3,128]{2,1,0:T(4,128)S(1)} %get-tuple-element.413), kind=kLoop, calls=%fused_computation.13.clone.1 | loop fusion | flops 9412608 | bytes 4489216 | tf_op jit(solution)/shard_map/while/body/eval_jaxpr/reduce_sum | solution.py:115
  557.8 8.9 %fusion.455 = f32[64,3,128]{2,1,0:T(4,128)S(1)} fusion(f32[64,128,128]{2,1,0:T(8,128)} %get-tuple-element.385, f32[64,3,128]{2,1,0:T(4,128)S(1)} %gather_fusion, f32[64,3,128]{2,1,0:T(4,128)S(1)} %get-tuple-element.413), kind=kLoop, calls=%fused_computation.13.clone.1 | loop fusion | flops 9412608 | bytes 4489216 | tf_op jit(solution)/shard_map/while/body/eval_jaxpr/reduce_sum | solution.py:115
  582.1 8.9 %fusion.455 = f32[64,3,128]{2,1,0:T(4,128)S(1)} fusion(f32[64,128,128]{2,1,0:T(8,128)} %get-tuple-element.385, f32[64,3,128]{2,1,0:T(4,128)S(1)} %gather_fusion, f32[64,3,128]{2,1,0:T(4,128)S(1)} %get-tuple-element.413), kind=kLoop, calls=%fused_computation.13.clone.1 | loop fusion | flops 9412608 | bytes 4489216 | tf_op jit(solution)/shard_map/while/body/eval_jaxpr/reduce_sum | solution.py:115
  606.3 8.9 %fusion.455 = f32[64,3,128]{2,1,0:T(4,128)S(1)} fusion(f32[64,128,128]{2,1,0:T(8,128)} %get-tuple-element.385, f32[64,3,128]{2,1,0:T(4,128)S(1)} %gather_fusion, f32[64,3,128]{2,1,0:T(4,128)S(1)} %get-tuple-element.413), kind=kLoop, calls=%fused_computation.13.clone.1 | loop fusion | flops 9412608 | bytes 4489216 | tf_op jit(solution)/shard_map/while/body/eval_jaxpr/reduce_sum | solution.py:115
  630.6 8.9 %fusion.455 = f32[64,3,128]{2,1,0:T(4,128)S(1)} fusion(f32[64,128,128]{2,1,0:T(8,128)} %get-tuple-element.385, f32[64,3,128]{2,1,0:T(4,128)S(1)} %gather_fusion, f32[64,3,128]{2,1,0:T(4,128)S(1)} %get-tuple-element.413), kind=kLoop, calls=%fused_computation.13.clone.1 | loop fusion | flops 9412608 | bytes 4489216 | tf_op jit(solution)/shard_map/while/body/eval_jaxpr/reduce_sum | solution.py:115
  654.9 8.9 %fusion.455 = f32[64,3,128]{2,1,0:T(4,128)S(1)} fusion(f32[64,128,128]{2,1,0:T(8,128)} %get-tuple-element.385, f32[64,3,128]{2,1,0:T(4,128)S(1)} %gather_fusion, f32[64,3,128]{2,1,0:T(4,128)S(1)} %get-tuple-element.413), kind=kLoop, calls=%fused_computation.13.clone.1 | loop fusion | flops 9412608 | bytes 4489216 | tf_op jit(solution)/shard_map/while/body/eval_jaxpr/reduce_sum | solution.py:115
  679.1 8.9 %fusion.455 = f32[64,3,128]{2,1,0:T(4,128)S(1)} fusion(f32[64,128,128]{2,1,0:T(8,128)} %get-tuple-element.385, f32[64,3,128]{2,1,0:T(4,128)S(1)} %gather_fusion, f32[64,3,128]{2,1,0:T(4,128)S(1)} %get-tuple-element.413), kind=kLoop, calls=%fused_computation.13.clone.1 | loop fusion | flops 9412608 | bytes 4489216 | tf_op jit(solution)/shard_map/while/body/eval_jaxpr/reduce_sum | solution.py:115
  703.4 8.9 %fusion.455 = f32[64,3,128]{2,1,0:T(4,128)S(1)} fusion(f32[64,128,128]{2,1,0:T(8,128)} %get-tuple-element.385, f32[64,3,128]{2,1,0:T(4,128)S(1)} %gather_fusion, f32[64,3,128]{2,1,0:T(4,128)S(1)} %get-tuple-element.413), kind=kLoop, calls=%fused_computation.13.clone.1 | loop fusion | flops 9412608 | bytes 4489216 | tf_op jit(solution)/shard_map/while/body/eval_jaxpr/reduce_sum | solution.py:115
  727.7 8.9 %fusion.455 = f32[64,3,128]{2,1,0:T(4,128)S(1)} fusion(f32[64,128,128]{2,1,0:T(8,128)} %get-tuple-element.385, f32[64,3,128]{2,1,0:T(4,128)S(1)} %gather_fusion, f32[64,3,128]{2,1,0:T(4,128)S(1)} %get-tuple-element.413), kind=kLoop, calls=%fused_computation.13.clone.1 | loop fusion | flops 9412608 | bytes 4489216 | tf_op jit(solution)/shard_map/while/body/eval_jaxpr/reduce_sum | solution.py:115
  751.9 8.9 %fusion.455 = f32[64,3,128]{2,1,0:T(4,128)S(1)} fusion(f32[64,128,128]{2,1,0:T(8,128)} %get-tuple-element.385, f32[64,3,128]{2,1,0:T(4,128)S(1)} %gather_fusion, f32[64,3,128]{2,1,0:T(4,128)S(1)} %get-tuple-element.413), kind=kLoop, calls=%fused_computation.13.clone.1 | loop fusion | flops 9412608 | bytes 4489216 | tf_op jit(solution)/shard_map/while/body/eval_jaxpr/reduce_sum | solution.py:115
  776.2 8.9 %fusion.455 = f32[64,3,128]{2,1,0:T(4,128)S(1)} fusion(f32[64,128,128]{2,1,0:T(8,128)} %get-tuple-element.385, f32[64,3,128]{2,1,0:T(4,128)S(1)} %gather_fusion, f32[64,3,128]{2,1,0:T(4,128)S(1)} %get-tuple-element.413), kind=kLoop, calls=%fused_computation.13.clone.1 | loop fusion | flops 9412608 | bytes 4489216 | tf_op jit(solution)/shard_map/while/body/eval_jaxpr/reduce_sum | solution.py:115
  (874 shorter events, 544.3 us)
Async XLA Ops:
  40.9 36.7 %copy-start.1 = (f32[64,128]{1,0:T(8,128)S(1)}, f32[64,128]{1,0:T(8,128)}, u32[]{:S(2)}) copy-start(f32[64,128]{1,0:T(8,128)} %param.11) | copy-start | bytes 98308
  64.2 27.5 %copy-start.4 = (s32[1,2,32]{2,1,0:T(2,128)S(1)}, s32[1,2,32]{2,1,0:T(2,128)}, u32[]{:S(2)}) copy-start(s32[1,2,32]{2,1,0:T(2,128)} %param.12) | copy-start | bytes 772
  65.5 26.9 %copy-start = (f32[64,3,128]{2,0,1:T(8,128)S(1)}, f32[64,3,128]{2,0,1:T(8,128)}, u32[]{:S(2)}) copy-start(f32[64,3,128]{2,0,1:T(8,128)} %param.10) | copy-start | bytes 294916
  74.4 23.4 %copy-start.5 = (s32[1,2,32]{2,1,0:T(2,128)S(1)}, s32[1,2,32]{2,1,0:T(2,128)}, u32[]{:S(2)}) copy-start(s32[1,2,32]{2,1,0:T(2,128)} %param.13) | copy-start | bytes 772
  74.4 23.5 %copy-start.3 = (s32[1,4,16]{2,1,0:T(4,128)S(1)}, s32[1,4,16]{2,1,0:T(4,128)}, u32[]{:S(2)}) copy-start(s32[1,4,16]{2,1,0:T(4,128)} %param.14) | copy-start | bytes 772
  80.8 28.9 %copy-start.2 = (s32[8,316]{1,0:T(8,128)S(1)}, s32[8,316]{1,0:T(8,128)}, u32[]{:S(2)}) copy-start(s32[8,316]{1,0:T(8,128)} %param.16) | copy-start | bytes 30340
  81.6 703.6 %all-to-all-start = ((bf16[128,121,8]{1,2,0:T(8,128)(2,1)}), bf16[128,121,8]{1,2,0:T(8,128)(2,1)S(1)}, u32[]{:S(2)}, u32[]{:S(2)}) async-start(bf16[128,121,8]{1,2,0:T(8,128)(2,1)} %stack.8), calls=%async_computation | async-start | bytes 524288 | tf_op jit(solution)/shard_map/all_to_all | solution.py:143
  93.5 16.5 %collective-permute-start = (f32[32,4,128]{2,1,0:T(4,128)S(1)}, f32[32,4,128]{2,1,0:T(4,128)S(1)}, u32[]{:S(2)}, u32[]{:S(2)}) collective-permute-start(f32[32,4,128]{2,1,0:T(4,128)S(1)} %get-tuple-element.310), channel_id=1, source_target_pairs={{0,32},{32,64},{64,96},{1,33},{33,65},{65,97},{2,34},{34,66},{66,9... | collective-permute-start | bytes 196616 | tf_op jit(solution)/shard_map/ppermute | solution.py:20
  96.6 17.5 %collective-permute-start.1 = (f32[32,4,128]{2,1,0:T(4,128)S(1)}, f32[32,4,128]{2,1,0:T(4,128)S(1)}, u32[]{:S(2)}, u32[]{:S(2)}) collective-permute-start(f32[32,4,128]{2,1,0:T(4,128)S(1)} %get-tuple-element.309), channel_id=1, source_target_pairs={{32,0},{64,32},{96,64},{33,1},{65,33},{97,65},{34,2},{66,34},{98,6... | collective-permute-start | bytes 196616 | tf_op jit(solution)/shard_map/ppermute | solution.py:20
  99.8 19.2 %collective-permute-start.2 = (f32[32,4,128]{2,1,0:T(4,128)S(1)}, f32[32,4,128]{2,1,0:T(4,128)S(1)}, u32[]{:S(2)}, u32[]{:S(2)}) collective-permute-start(f32[32,4,128]{2,1,0:T(4,128)S(1)} %get-tuple-element.308), channel_id=1, source_target_pairs={{0,1},{1,2},{2,3},{3,4},{4,5},{5,6},{6,7},{7,8},{8,9},{9,10},{10,1... | collective-permute-start | bytes 196616 | tf_op jit(solution)/shard_map/ppermute | solution.py:20
  101.1 19.4 %collective-permute-start.3 = (f32[32,4,128]{2,1,0:T(4,128)S(1)}, f32[32,4,128]{2,1,0:T(4,128)S(1)}, u32[]{:S(2)}, u32[]{:S(2)}) collective-permute-start(f32[32,4,128]{2,1,0:T(4,128)S(1)} %get-tuple-element.307), channel_id=1, source_target_pairs={{1,0},{2,1},{3,2},{4,3},{5,4},{6,5},{7,6},{8,7},{9,8},{10,9},{11,1... | collective-permute-start | bytes 196616 | tf_op jit(solution)/shard_map/ppermute | solution.py:20
  105.9 14.6 %collective-permute-start.4 = (f32[16,4,128]{2,1,0:T(4,128)S(1)}, f32[16,4,128]{2,1,0:T(4,128)S(1)}, u32[]{:S(2)}, u32[]{:S(2)}) collective-permute-start(f32[16,4,128]{2,1,0:T(4,128)S(1)} %get-tuple-element.304), channel_id=1, source_target_pairs={{0,33},{1,34},{2,35},{3,36},{4,37},{5,38},{6,39},{7,40},{8,41},{9,... | collective-permute-start | bytes 98312 | tf_op jit(solution)/shard_map/ppermute | solution.py:20
  110.0 10.5 %collective-permute-start.5 = (f32[16,4,128]{2,1,0:T(4,128)S(1)}, f32[16,4,128]{2,1,0:T(4,128)S(1)}, u32[]{:S(2)}, u32[]{:S(2)}) collective-permute-start(f32[16,4,128]{2,1,0:T(4,128)S(1)} %get-tuple-element.305), channel_id=1, source_target_pairs={{0,31},{1,32},{2,33},{3,34},{4,35},{5,36},{6,37},{7,38},{8,39},{9,... | collective-permute-start | bytes 98312 | tf_op jit(solution)/shard_map/ppermute | solution.py:20
  114.1 6.8 collective-permute-start.6
  118.9 11.0 %collective-permute-start.7 = (f32[16,4,128]{2,1,0:T(4,128)S(1)}, f32[16,4,128]{2,1,0:T(4,128)S(1)}, u32[]{:S(2)}, u32[]{:S(2)}) collective-permute-start(f32[16,4,128]{2,1,0:T(4,128)S(1)} %get-tuple-element.303), channel_id=1, source_target_pairs={{33,0},{34,1},{35,2},{36,3},{37,4},{38,5},{39,6},{40,7},{41,8},{42... | collective-permute-start | bytes 98312 | tf_op jit(solution)/shard_map/ppermute | solution.py:20
